TPU v7x, 512 devices: a whole 4x8x8 slice. The times are simulated.
512 devices in a mesh: dp: 16 (over z, core), seq: 32 (over x, y).
Axes of the slice: x: 4, y: 8, z: 8, core: 2. Of those that a mesh axis runs over, the one named last changes fastest.
Arguments:
- queries: bfloat16 [65536, 4096], P(('dp', 'seq')), may hold values from -6 to 6
- keys: bfloat16 [65536, 512], P(('dp', 'seq')), may hold values from -6 to 6
- values: bfloat16 [65536, 512], P(('dp', 'seq')), may hold values from -6 to 6
- d_out: bfloat16 [65536, 4096], P(('dp', 'seq')), may hold values from -6 to 6
- doc_lengths: int32 [171], replicated, may hold values from 1 to 768, as said below
Outputs:
- d_queries: bfloat16 [65536, 4096], P(('dp', 'seq'))
- key_gradient: bfloat16 [65536, 512], P(('dp', 'seq'))
- value_gradient: bfloat16 [65536, 512], P(('dp', 'seq'))
Inputs may be any that keep to these rules, and one draw needn't show every extreme that they name: `doc_lengths`: lengths of the 171 documents in order; they sum to 65536, and the longest has exactly 768 tokens.
All inputs are finite; a program needn't handle non-finite values.
Results may differ from a plain program's by a relative error of at most 0.008.
Values may be sent and summed in bfloat16 or wider, within the bound.
A program may use at most 64 MiB of HBM per device.

v0:
```python
import math

import jax
import jax.numpy as jnp
from jax import lax
from jax.sharding import PartitionSpec as P

HEAD_SIZE = 128
GROUP = 8
DOC_MOST = 768


def from_behind(value, axis, steps):
    count = lax.axis_size(axis)
    leading, last = (max(0, -steps), min(count, count - steps))
    return lax.ppermute(value, axis, [(source, source + steps) for source in range(leading, last)])


def as_sent(shard):
    return jax.tree.map(lambda a: a.astype(jnp.bfloat16) if a.dtype == jnp.float32 else a, shard)


def doc_index(positions, doc_ends):
    return jnp.sum((positions[:, None] >= doc_ends[None, :]).astype(jnp.int32), axis=1)


def block_grads(q_rows, key_rows, value_rows, grad_rows, allowed, score_scale):
    scores = jnp.dot(q_rows, key_rows.T, preferred_element_type=jnp.float32) * score_scale
    scores = jnp.where(allowed, scores, -1e30)
    row_max = jnp.max(scores, axis=1, keepdims=True)
    exp_scores = jnp.exp(scores - row_max)
    attn_probs = exp_scores / jnp.sum(exp_scores, axis=1, keepdims=True)
    probs_low = attn_probs.astype(jnp.bfloat16)
    grad_probs = jnp.dot(grad_rows, value_rows.T, preferred_element_type=jnp.float32)
    row_delta = jnp.sum(attn_probs * grad_probs, axis=1, keepdims=True)
    grad_scores = (attn_probs * (grad_probs - row_delta) * score_scale).astype(jnp.bfloat16)
    grad_q = jnp.dot(grad_scores, key_rows, preferred_element_type=jnp.float32)
    grad_k = jnp.dot(grad_scores.T, q_rows, preferred_element_type=jnp.float32)
    grad_v = jnp.dot(probs_low.T, grad_rows, preferred_element_type=jnp.float32)
    return (grad_q, grad_k, grad_v)


def local(queries, keys, values, d_out, doc_lengths):
    tok_rows, q_width = queries.shape
    seq_devices = lax.axis_size("seq")
    kv_width = keys.shape[1]
    kv_heads = kv_width // HEAD_SIZE
    doc_ends = jnp.cumsum(doc_lengths)
    score_scale = 1.0 / math.sqrt(HEAD_SIZE)
    block_rows = tok_rows * seq_devices
    spread_k = jnp.broadcast_to(
        keys.reshape(tok_rows, kv_heads, 1, HEAD_SIZE), (tok_rows, kv_heads, GROUP, HEAD_SIZE)
    ).reshape(tok_rows, q_width)
    spread_v = jnp.broadcast_to(
        values.reshape(tok_rows, kv_heads, 1, HEAD_SIZE), (tok_rows, kv_heads, GROUP, HEAD_SIZE)
    ).reshape(tok_rows, q_width)
    head_q, head_g, head_k, head_v = (
        lax.all_to_all(queries, "seq", split_axis=1, concat_axis=0, tiled=True),
        lax.all_to_all(d_out, "seq", split_axis=1, concat_axis=0, tiled=True),
        lax.all_to_all(spread_k, "seq", split_axis=1, concat_axis=0, tiled=True),
        lax.all_to_all(spread_v, "seq", split_axis=1, concat_axis=0, tiled=True),
    )
    tail_pair = jnp.stack([head_k, head_v])
    prior_pair = from_behind(tail_pair, "dp", 1)
    all_k = jnp.concatenate([prior_pair[0], head_k], axis=0)
    all_v = jnp.concatenate([prior_pair[1], head_v], axis=0)
    block_start = lax.axis_index("dp") * block_rows
    query_span = min(512, block_rows)
    key_window = query_span + DOC_MOST
    steps_count = block_rows // query_span
    query_pos = block_start + jnp.arange(block_rows, dtype=jnp.int32)
    key_pos = block_start - block_rows + jnp.arange(block_rows + block_rows, dtype=jnp.int32)
    query_docs = doc_index(query_pos, doc_ends)
    key_docs = doc_index(key_pos, doc_ends)

    def step(totals, step_index):
        acc_k, acc_v = totals
        row_start = step_index * query_span
        key_start = row_start + block_rows - DOC_MOST
        q_rows = lax.dynamic_slice_in_dim(head_q, row_start, query_span, 0)
        g_rows = lax.dynamic_slice_in_dim(head_g, row_start, query_span, 0)
        key_rows = lax.dynamic_slice_in_dim(all_k, key_start, key_window, 0)
        value_rows = lax.dynamic_slice_in_dim(all_v, key_start, key_window, 0)
        q_pos = lax.dynamic_slice_in_dim(query_pos, row_start, query_span, 0)
        k_pos = lax.dynamic_slice_in_dim(key_pos, key_start, key_window, 0)
        q_docs = lax.dynamic_slice_in_dim(query_docs, row_start, query_span, 0)
        k_docs = lax.dynamic_slice_in_dim(key_docs, key_start, key_window, 0)
        allowed = (
            (q_docs[:, None] == k_docs[None, :])
            & (k_pos[None, :] <= q_pos[:, None])
            & (k_pos[None, :] >= 0)
        )
        grad_q, grad_k, grad_v = block_grads(
            q_rows, key_rows, value_rows, g_rows, allowed, score_scale
        )
        acc_k = lax.dynamic_update_slice_in_dim(
            acc_k, lax.dynamic_slice_in_dim(acc_k, key_start, key_window, 0) + grad_k, key_start, 0
        )
        acc_v = lax.dynamic_update_slice_in_dim(
            acc_v, lax.dynamic_slice_in_dim(acc_v, key_start, key_window, 0) + grad_v, key_start, 0
        )
        return ((acc_k, acc_v), grad_q.astype(jnp.bfloat16))

    empty_acc = jnp.zeros((block_rows + block_rows, HEAD_SIZE), jnp.float32)
    (acc_k, acc_v), q_blocks = lax.scan(
        step, (empty_acc, empty_acc), jnp.arange(steps_count, dtype=jnp.int32)
    )
    grads_q = q_blocks.reshape(block_rows, HEAD_SIZE)
    back_pair = from_behind(
        jnp.stack([acc_k[:block_rows], acc_v[:block_rows]]).astype(jnp.bfloat16), "dp", -1
    ).astype(jnp.float32)
    own_k = acc_k[block_rows:]
    own_v = acc_v[block_rows:]
    split_at = block_rows - block_rows
    term_k = jnp.concatenate([own_k[:split_at], own_k + back_pair[0]], axis=0)
    term_v = jnp.concatenate([own_v[:split_at], own_v + back_pair[1]], axis=0)
    tok_dq = lax.all_to_all(grads_q, "seq", split_axis=0, concat_axis=1, tiled=True)
    tok_k, tok_v = (
        lax.all_to_all(as_sent(term_k), "seq", split_axis=0, concat_axis=1, tiled=True).astype(
            term_k.dtype
        ),
        lax.all_to_all(as_sent(term_v), "seq", split_axis=0, concat_axis=1, tiled=True).astype(
            term_v.dtype
        ),
    )
    key_gradient = (
        jnp.sum(tok_k.reshape(tok_rows, kv_heads, GROUP, HEAD_SIZE), axis=2)
        .reshape(tok_rows, kv_width)
        .astype(jnp.bfloat16)
    )
    value_gradient = (
        jnp.sum(tok_v.reshape(tok_rows, kv_heads, GROUP, HEAD_SIZE), axis=2)
        .reshape(tok_rows, kv_width)
        .astype(jnp.bfloat16)
    )
    return (tok_dq, key_gradient, value_gradient)


def solution(mesh):
    in_specs = (
        P(("dp", "seq"), None),
        P(("dp", "seq"), None),
        P(("dp", "seq"), None),
        P(("dp", "seq"), None),
        P(),
    )
    out_specs = (P(("dp", "seq"), None), P(("dp", "seq"), None), P(("dp", "seq"), None))
    return jax.shard_map(local, mesh=mesh, in_specs=in_specs, out_specs=out_specs, check_vma=False)
```

profile of v0, /device:TPU:448, one launch (start us, length us, event | category | flops | bytes accessed | tf_op | source)
XLA Modules:
  0.0 370.4 jit_solution(15627165320955770170)
XLA Ops:
  2.9 10.0 %all-to-all-start.2 = ((bf16[128,32,128]{2,0,1:T(8,128)(2,1)}), bf16[128,32,128]{2,0,1:T(8,128)(2,1)S(1)}, u32[]{:S(2)}, u32[]{:S(2)}) async-start(bf16[128,32,128]{2,0,1:T(8,128)(2,1)} %bitcast.9), calls=%async_computation.2 | async-start | bytes 2097152 | tf_op jit(solution)/shard_map/all_to_all | solution.py:61
  12.9 28.6 %all-to-all-done.2 = bf16[128,32,128]{2,0,1:T(8,128)(2,1)S(1)} async-done(((bf16[128,32,128]{2,0,1:T(8,128)(2,1)}), bf16[128,32,128]{2,0,1:T(8,128)(2,1)S(1)}, u32[]{:S(2)}, u32[]{:S(2)}) %all-to-all-start.2) | async-done | bytes 1048608 | tf_op jit(solution)/shard_map/all_to_all | solution.py:61
  42.7 5.1 %all-to-all-start.1 = ((bf16[128,32,128]{2,0,1:T(8,128)(2,1)}), bf16[128,32,128]{2,0,1:T(8,128)(2,1)S(1)}, u32[]{:S(2)}, u32[]{:S(2)}) async-start(bf16[128,32,128]{2,0,1:T(8,128)(2,1)} %bitcast.99), calls=%async_computation.1 | async-start | bytes 2097152 | tf_op jit(solution)/shard_map/all_to_all | solution.py:60
  49.1 27.0 %all-to-all-done.1 = bf16[128,32,128]{2,0,1:T(8,128)(2,1)S(1)} async-done(((bf16[128,32,128]{2,0,1:T(8,128)(2,1)}), bf16[128,32,128]{2,0,1:T(8,128)(2,1)S(1)}, u32[]{:S(2)}, u32[]{:S(2)}) %all-to-all-start.1) | async-done | bytes 1048608 | tf_op jit(solution)/shard_map/all_to_all | solution.py:60
  76.1 5.0 %all-to-all-start = ((bf16[128,32,128]{2,0,1:T(8,128)(2,1)}), bf16[128,32,128]{2,0,1:T(8,128)(2,1)}, u32[]{:S(2)}, u32[]{:S(2)}) async-start(bf16[128,32,128]{2,0,1:T(8,128)(2,1)} %copy_bitcast_fusion.1), calls=%async_computation | async-start | bytes 2097152 | tf_op jit(solution)/shard_map/all_to_all | solution.py:58
  86.0 2.5 copy_bitcast_fusion
  88.5 21.0 %all-to-all-done = bf16[128,32,128]{2,0,1:T(8,128)(2,1)} async-done(((bf16[128,32,128]{2,0,1:T(8,128)(2,1)}), bf16[128,32,128]{2,0,1:T(8,128)(2,1)}, u32[]{:S(2)}, u32[]{:S(2)}) %all-to-all-start) | async-done | bytes 1048608 | tf_op jit(solution)/shard_map/all_to_all | solution.py:58
  109.4 5.0 %all-to-all-start.3 = ((bf16[128,32,128]{2,0,1:T(8,128)(2,1)}), bf16[128,32,128]{2,0,1:T(8,128)(2,1)}, u32[]{:S(2)}, u32[]{:S(2)}) async-start(bf16[128,32,128]{2,0,1:T(8,128)(2,1)} %copy_bitcast_fusion), calls=%async_computation.3 | async-start | bytes 2097152 | tf_op jit(solution)/shard_map/all_to_all | solution.py:59
  116.6 2.2 pad_maximum_fusion.1
  118.8 23.9 %all-to-all-done.3 = bf16[128,32,128]{2,0,1:T(8,128)(2,1)} async-done(((bf16[128,32,128]{2,0,1:T(8,128)(2,1)}), bf16[128,32,128]{2,0,1:T(8,128)(2,1)}, u32[]{:S(2)}, u32[]{:S(2)}) %all-to-all-start.3) | async-done | bytes 1048608 | tf_op jit(solution)/shard_map/all_to_all | solution.py:59
  142.8 2.2 broadcast_in_dim.52.clone
  145.0 2.2 broadcast_in_dim.52
  147.2 113.3 %while.18 = (s32[]{:T(128)}, f32[8192,128]{1,0:T(8,128)}, f32[8192,128]{1,0:T(8,128)}, bf16[8,512,128]{2,1,0:T(8,128)(2,1)}, s32[8]{0:T(128)S(1)}, /*index=5*/s3...) while((s32[]{:T(128)}, f32[8192,128]{1,0:T(8,128)}, ...), condition=%wide.region_8.9_spmd, body=%wide.region_4.0_spmd.sunk | while | flops 853671680 | bytes 26610516 | solution.py:105
  153.9 2.1 fusion.56
  156.0 2.8 fusion.55
  158.8 2.6 fusion.54
  162.9 2.0 fusion.52
  168.0 2.1 fusion.56
  170.2 2.8 fusion.55
  173.0 2.5 fusion.54
  182.2 2.1 fusion.56
  184.4 2.8 fusion.55
  187.1 2.6 fusion.54
  196.4 2.1 fusion.56
  198.5 2.8 fusion.55
  201.3 2.6 fusion.54
  210.6 2.1 fusion.56
  212.7 2.8 fusion.55
  215.5 2.6 fusion.54
  219.6 2.0 fusion.52
  224.7 2.1 fusion.56
  226.9 2.8 fusion.55
  229.7 2.5 fusion.54
  233.8 2.0 fusion.52
  238.9 2.1 fusion.56
  241.0 2.8 fusion.55
  243.8 2.5 fusion.54
  253.0 2.1 fusion.56
  255.2 2.8 fusion.55
  258.0 2.6 fusion.54
  267.4 4.9 %all-to-all-start.4 = ((bf16[32,128,128]{2,1,0:T(8,128)(2,1)}), bf16[32,128,128]{2,1,0:T(8,128)(2,1)S(1)}, u32[]{:S(2)}, u32[]{:S(2)}) async-start(bf16[32,128,128]{2,1,0:T(8,128)(2,1)} %bitcast.18), calls=%async_computation.4 | async-start | bytes 2097152 | tf_op jit(solution)/shard_map/all_to_all | solution.py:117
  272.3 18.9 %collective-permute-done.1 = bf16[2,4096,128]{2,1,0:T(8,128)(2,1)} collective-permute-done((bf16[2,4096,128]{2,1,0:T(8,128)(2,1)}, bf16[2,4096,128]{2,1,0:T(8,128)(2,1)}, u32[]{:S(2)}, u32[]{:S(2)}) %collective-permute-start.1) | collective-permute-done | bytes 2097184 | tf_op jit(solution)/shard_map/ppermute | solution.py:16
  293.1 3.2 fusion.23
  296.3 3.9 %all-to-all-done.4 = bf16[32,128,128]{2,1,0:T(8,128)(2,1)S(1)} async-done(((bf16[32,128,128]{2,1,0:T(8,128)(2,1)}), bf16[32,128,128]{2,1,0:T(8,128)(2,1)S(1)}, u32[]{:S(2)}, u32[]{:S(2)}) %all-to-all-start.4) | async-done | bytes 1048608 | tf_op jit(solution)/shard_map/all_to_all | solution.py:117
  300.2 35.8 %all_to_all.121 = bf16[32,128,128]{2,1,0:T(8,128)(2,1)} all-to-all(bf16[32,128,128]{2,1,0:T(8,128)(2,1)S(1)} %bitcast.98), channel_id=1, replica_groups=mesh['dp'=16,'seq'=32] {'seq'}, dimensions={0} | all-to-all | bytes 2097152 | tf_op jit(solution)/shard_map/all_to_all | solution.py:119
  336.0 5.1 %all-to-all-start.6 = ((bf16[32,128,128]{2,1,0:T(8,128)(2,1)}), bf16[32,128,128]{2,1,0:T(8,128)(2,1)S(1)}, u32[]{:S(2)}, u32[]{:S(2)}) async-start(bf16[32,128,128]{2,1,0:T(8,128)(2,1)} %bitcast.29), calls=%async_computation.6 | async-start | bytes 2097152 | tf_op jit(solution)/shard_map/all_to_all | solution.py:122
  342.5 2.4 copy.39
  345.9 23.5 %all-to-all-done.6 = bf16[32,128,128]{2,1,0:T(8,128)(2,1)S(1)} async-done(((bf16[32,128,128]{2,1,0:T(8,128)(2,1)}), bf16[32,128,128]{2,1,0:T(8,128)(2,1)S(1)}, u32[]{:S(2)}, u32[]{:S(2)}) %all-to-all-start.6) | async-done | bytes 1048608 | tf_op jit(solution)/shard_map/all_to_all | solution.py:122
  (112 shorter events, 65.7 us)
Async XLA Ops:
  0.6 47.2 %copy-start = (bf16[128,4096]{1,0:T(8,128)(2,1)S(1)}, bf16[128,4096]{1,0:T(8,128)(2,1)}, u32[]{:S(2)}) copy-start(bf16[128,4096]{1,0:T(8,128)(2,1)} %param.7) | copy-start | bytes 3145732
  0.6 12.2 %copy-start.3 = (bf16[128,512]{1,0:T(8,128)(2,1)S(1)}, bf16[128,512]{1,0:T(8,128)(2,1)}, u32[]{:S(2)}) copy-start(bf16[128,512]{1,0:T(8,128)(2,1)} %param.8) | copy-start | bytes 393220
  2.9 38.6 %all-to-all-start.2 = ((bf16[128,32,128]{2,0,1:T(8,128)(2,1)}), bf16[128,32,128]{2,0,1:T(8,128)(2,1)S(1)}, u32[]{:S(2)}, u32[]{:S(2)}) async-start(bf16[128,32,128]{2,0,1:T(8,128)(2,1)} %bitcast.9), calls=%async_computation.2 | async-start | bytes 2097152 | tf_op jit(solution)/shard_map/all_to_all | solution.py:61
  42.7 33.4 %all-to-all-start.1 = ((bf16[128,32,128]{2,0,1:T(8,128)(2,1)}), bf16[128,32,128]{2,0,1:T(8,128)(2,1)S(1)}, u32[]{:S(2)}, u32[]{:S(2)}) async-start(bf16[128,32,128]{2,0,1:T(8,128)(2,1)} %bitcast.99), calls=%async_computation.1 | async-start | bytes 2097152 | tf_op jit(solution)/shard_map/all_to_all | solution.py:60
  76.1 33.3 %all-to-all-start = ((bf16[128,32,128]{2,0,1:T(8,128)(2,1)}), bf16[128,32,128]{2,0,1:T(8,128)(2,1)}, u32[]{:S(2)}, u32[]{:S(2)}) async-start(bf16[128,32,128]{2,0,1:T(8,128)(2,1)} %copy_bitcast_fusion.1), calls=%async_computation | async-start | bytes 2097152 | tf_op jit(solution)/shard_map/all_to_all | solution.py:58
  81.1 3.5 copy-start.4
  82.7 32.2 %collective-permute-start = (bf16[2,4096,128]{2,1,0:T(8,128)(2,1)}, bf16[2,4096,128]{2,1,0:T(8,128)(2,1)}, u32[]{:S(2)}, u32[]{:S(2)}) collective-permute-start(bf16[2,4096,128]{2,1,0:T(8,128)(2,1)} %pad_maximum_fusion), channel_id=1, source_target_pairs={{0,32},{32,64},{64,96},{96,128},{128,160},{160,192},{192,224},{224... | collective-permute-start | bytes 6291464 | tf_op jit(solution)/shard_map/ppermute | solution.py:16
  109.4 33.3 %all-to-all-start.3 = ((bf16[128,32,128]{2,0,1:T(8,128)(2,1)}), bf16[128,32,128]{2,0,1:T(8,128)(2,1)}, u32[]{:S(2)}, u32[]{:S(2)}) async-start(bf16[128,32,128]{2,0,1:T(8,128)(2,1)} %copy_bitcast_fusion), calls=%async_computation.3 | async-start | bytes 2097152 | tf_op jit(solution)/shard_map/all_to_all | solution.py:59
  265.5 25.8 %collective-permute-start.1 = (bf16[2,4096,128]{2,1,0:T(8,128)(2,1)}, bf16[2,4096,128]{2,1,0:T(8,128)(2,1)}, u32[]{:S(2)}, u32[]{:S(2)}) collective-permute-start(bf16[2,4096,128]{2,1,0:T(8,128)(2,1)} %pad_maximum_fusion.3), channel_id=1, source_target_pairs={{32,0},{64,32},{96,64},{128,96},{160,128},{192,160},{224,192},{256... | collective-permute-start | bytes 6291464 | tf_op jit(solution)/shard_map/ppermute | solution.py:16
  267.4 32.8 %all-to-all-start.4 = ((bf16[32,128,128]{2,1,0:T(8,128)(2,1)}), bf16[32,128,128]{2,1,0:T(8,128)(2,1)S(1)}, u32[]{:S(2)}, u32[]{:S(2)}) async-start(bf16[32,128,128]{2,1,0:T(8,128)(2,1)} %bitcast.18), calls=%async_computation.4 | async-start | bytes 2097152 | tf_op jit(solution)/shard_map/all_to_all | solution.py:117
  272.3 20.8 %copy-start.1 = (f32[8192,128]{1,0:T(8,128)S(1)}, f32[8192,128]{1,0:T(8,128)}, u32[]{:S(2)}) copy-start(f32[8192,128]{1,0:T(8,128)} %get-tuple-element.261) | copy-start | bytes 12582916
  336.0 33.4 %all-to-all-start.6 = ((bf16[32,128,128]{2,1,0:T(8,128)(2,1)}), bf16[32,128,128]{2,1,0:T(8,128)(2,1)S(1)}, u32[]{:S(2)}, u32[]{:S(2)}) async-start(bf16[32,128,128]{2,1,0:T(8,128)(2,1)} %bitcast.29), calls=%async_computation.6 | async-start | bytes 2097152 | tf_op jit(solution)/shard_map/all_to_all | solution.py:122
  342.5 2.4 copy-start.2
where the time goes:
time: 373 us; the launch traced here: 370 us
  waiting for transfers between devices  147 us (39%)
  matrix products  90.5 us (24%)
  starting transfers between devices  38.9 us (10%)
  blocking collectives  35.8 us (10%)
  local copies, waits for them, and re-layouts  29 us (8%)
  other arithmetic  23.1 us (6%)
  loops' own time  5.39 us (1%)
    all_to_all x1, blocking collectives, local(): lax.all_to_all(as_sent(term_k), 'seq', split_axis=0, concat_axis=1, tiled...  35.8 us
    all_to_all x1, waiting for transfers between devices, local(): lax.all_to_all(spread_v, 'seq', split_axis=1, concat_axis=0, tiled=True)  28.6 us
    all_to_all x1, waiting for transfers between devices, local(): lax.all_to_all(spread_k, 'seq', split_axis=1, concat_axis=0, tiled=True)  27 us
    all_to_all x1, waiting for transfers between devices, local(): lax.all_to_all(d_out, 'seq', split_axis=1, concat_axis=0, tiled=True)  23.9 us
    all_to_all x1, waiting for transfers between devices, local(): lax.all_to_all(as_sent(term_v), 'seq', split_axis=0, concat_axis=1, tiled...  23.5 us
    dot_general x8, matrix products, block_grads(): grad_v = jnp.dot(probs_low.T, grad_rows, preferred_element_type=jnp.float32)  22.3 us
    all_to_all x1, waiting for transfers between devices, local(): lax.all_to_all(queries, 'seq', split_axis=1, concat_axis=0, tiled=True)  21 us
    dot_general x8, matrix products, block_grads(): grad_k = jnp.dot(grad_scores.T, q_rows, preferred_element_type=jnp.float32)  20.4 us
  transfers between devices with their start and end apart: 8, of which 7 were waited for; matrix products, arithmetic and copies ran while one was open for 6% of the time, Pallas kernels for 0%

commit v1 on v0

v1 whole, which is shorter than its diff:
```python
import functools
import math

import jax
import jax.numpy as jnp
from jax import lax
from jax.experimental import pallas as pl
from jax.experimental.pallas import tpu as pltpu
from jax.sharding import PartitionSpec as P

HEAD = 128
GROUP = 8
ROWS = 128
BACK = 6
SLOTS = BACK + 1
PAIRS = GROUP // 2
MESH = pl.DeviceIdType.MESH
NEG = -1e30
CONTRACT_LAST = (((1,), (1,)), ((), ()))


def near_of(g):
    return 4 if g % 2 == 0 else 3


def kernel(
    kv_heads, n_dp, n_seq,
    q_hbm, k_hbm, v_hbm, go_hbm, len_ref,
    dq_ref, dk_ref, dv_ref,
    q_ref, go_ref, kv, kt, bias, s_ref, g_ref, part, out_buf, in_buf,
    load_sem, own_sem, kv_send, kv_recv, d_send, d_recv,
):
    total = n_dp * n_seq
    me = lax.axis_index("dp") * n_seq + lax.axis_index("seq")

    def device(offset):
        there = lax.rem(me + (offset + total), total)
        return (there // n_seq, lax.rem(there, n_seq))

    own = []
    for g in range(kv_heads):
        for which, ref in ((0, k_hbm), (1, v_hbm)):
            own.append(pltpu.make_async_copy(
                ref.at[:, pl.ds(g * HEAD, HEAD)], kv.at[g, which, 0], own_sem.at[g, which]))
            own[-1].start()
    load_q = pltpu.make_async_copy(q_hbm, q_ref, load_sem.at[0])
    load_go = pltpu.make_async_copy(go_hbm, go_ref, load_sem.at[1])
    load_q.start()
    load_go.start()

    barrier = pltpu.get_barrier_semaphore()
    partners = (1, -1, BACK, -BACK)
    for offset in partners:
        pl.semaphore_signal(barrier, inc=1, device_id=device(offset), device_id_type=MESH)

    lens = len_ref[...].astype(jnp.float32)
    n_len = lens.shape[1]
    j = lax.broadcasted_iota(jnp.int32, (n_len, n_len), 0)
    k = lax.broadcasted_iota(jnp.int32, (n_len, n_len), 1)
    ends = jnp.sum(jnp.where(k <= j, jnp.broadcast_to(lens, (n_len, n_len)), 0.0), axis=1, keepdims=True)
    q_pos = (me * ROWS + lax.broadcasted_iota(jnp.int32, (1, ROWS), 1)).astype(jnp.float32)
    first = jnp.max(jnp.where(ends <= q_pos, ends, 0.0), axis=0, keepdims=True)
    for d in range(SLOTS):
        k_pos = ((me - d) * ROWS + lax.broadcasted_iota(jnp.int32, (ROWS, ROWS), 0)).astype(jnp.float32)
        bias[d] = jnp.where((k_pos >= first) & (k_pos <= q_pos), 0.0, NEG)
    part[...] = jnp.zeros_like(part)

    pl.semaphore_wait(barrier, len(partners))

    def kv_copy(g, source, target):
        offset = {(0, BACK): BACK}.get((source, target), target - source)
        return pltpu.make_async_remote_copy(
            src_ref=kv.at[g, :, source], dst_ref=kv.at[g, :, target],
            send_sem=kv_send.at[g, target], recv_sem=kv_recv.at[g, target],
            device_id=device(offset), device_id_type=MESH)

    def kv_first(g):
        own[2 * g].wait()
        own[2 * g + 1].wait()
        kv_copy(g, 0, 1).start()
        kv_copy(g, 0, BACK).start()

    def kv_pass(g, hop):
        near, far = hop, BACK + 1 - hop
        if near <= near_of(g):
            kv_copy(g, near - 1, near).wait_recv()
            if near < near_of(g):
                kv_copy(g, near, near + 1).start()
        if far > near_of(g):
            kv_copy(g, 0 if far == BACK else far + 1, far).wait_recv()
            if far - 1 > near_of(g):
                kv_copy(g, far, far - 1).start()

    def d_copy(g, source, target, offset):
        return pltpu.make_async_remote_copy(
            src_ref=out_buf.at[g, source], dst_ref=in_buf.at[g, target],
            send_sem=d_send.at[g, source], recv_sem=d_recv.at[g, target],
            device_id=device(offset), device_id_type=MESH)

    def d_near(g, d):
        return d_copy(g, d, d - 1, -1)

    def d_far(g, d):
        return d_copy(g, d, d + 1, 1 if d < BACK else -BACK)

    def d_first(g):
        for d, copy in ((near_of(g), d_near), (near_of(g) + 1, d_far)):
            out_buf[g, d] = part[g, :, d].astype(jnp.bfloat16)
            copy(g, d).start()

    def d_pass(g, hop):
        d = near_of(g) - hop
        if d >= 1:
            d_near(g, d + 1).wait_recv()
            out_buf[g, d] = (part[g, :, d] + in_buf[g, d].astype(jnp.float32)).astype(jnp.bfloat16)
            d_near(g, d).start()
        d = near_of(g) + 1 + hop
        if d <= BACK:
            d_far(g, d - 1).wait_recv()
            out_buf[g, d] = (part[g, :, d] + in_buf[g, d].astype(jnp.float32)).astype(jnp.bfloat16)
            d_far(g, d).start()
        if hop == near_of(g):
            d_near(g, 1).wait_recv()
            d_far(g, BACK).wait_recv()
            done = part[g, :, 0] + in_buf[g, 0].astype(jnp.float32) + in_buf[g, BACK + 1].astype(jnp.float32)
            dk_ref[:, g * HEAD:(g + 1) * HEAD] = done[0].astype(jnp.bfloat16)
            dv_ref[:, g * HEAD:(g + 1) * HEAD] = done[1].astype(jnp.bfloat16)

    scale = 1.0 / math.sqrt(HEAD)
    exp_scale = scale / math.log(2.0)

    def flat(x):
        return x.reshape(SLOTS * ROWS, x.shape[-1])

    def heads_of(ref, at):
        return jnp.concatenate([ref[:, pl.ds(at, HEAD)], ref[:, pl.ds(at + HEAD, HEAD)]], axis=0)

    def pair(g, p):
        at = pl.multiple_of((g * PAIRS + p) * (2 * HEAD), 2 * HEAD)

        @pl.when(p == 0)
        def _():
            kt[...] = flat(kv[g, 0]).T

        q2, go2 = heads_of(q_ref, at), heads_of(go_ref, at)
        keys, vals = flat(kv[g, 0]), flat(kv[g, 1])
        off = flat(bias[...])
        s = lax.dot_general(keys, q2, CONTRACT_LAST, preferred_element_type=jnp.float32)
        s = s + jnp.concatenate([off, off], axis=1)
        s_ref[...] = s
        top = jnp.max(s, axis=0, keepdims=True)
        grads = lax.dot_general(vals, go2, CONTRACT_LAST, preferred_element_type=jnp.float32)
        g_ref[...] = grads
        e = jnp.exp2((s_ref[...] - top) * exp_scale)
        s_ref[...] = e
        inv = 1.0 / jnp.sum(e, axis=0, keepdims=True)
        delta = jnp.sum(e * grads, axis=0, keepdims=True) * inv
        e = s_ref[...]
        low = (e * inv).astype(jnp.bfloat16)
        ds = ((e * (inv * scale)) * (g_ref[...] - delta)).astype(jnp.bfloat16)
        dk = jnp.dot(ds, q2, preferred_element_type=jnp.float32)
        dv = jnp.dot(low, go2, preferred_element_type=jnp.float32)
        part[g, 0] += dk.reshape(SLOTS, ROWS, HEAD)
        part[g, 1] += dv.reshape(SLOTS, ROWS, HEAD)
        dq = jnp.dot(kt[...], ds, preferred_element_type=jnp.float32).T.astype(jnp.bfloat16)
        dq_ref[:, pl.ds(at, HEAD)] = dq[:ROWS]
        dq_ref[:, pl.ds(at + HEAD, HEAD)] = dq[ROWS:]

    n = kv_heads * PAIRS
    events = [(-9, kv_first, (0,)), (-9, kv_first, (1,))]
    for g in range(2):
        for hop in range(1, near_of(g) + 1):
            events.append((-9 + hop if g == 0 else -9 + hop + 0.5, kv_pass, (g, hop)))
    events.append((-6.5, kv_first, (2,)))
    events.append((-5.5, kv_first, (3,)))
    for g in range(2, kv_heads):
        for hop in range(1, near_of(g) + 1):
            events.append((2 * hop - 2 + (g - 2), kv_pass, (g, hop)))
    for g in range(kv_heads):
        events.append((PAIRS * (g + 1), d_first, (g,)))
        for hop in range(1, near_of(g) + 1):
            events.append((PAIRS * (g + 1) + 2 * hop, d_pass, (g, hop)))
    events.sort(key=lambda event: event[0])
    for when, what, which in events:
        if when < 0:
            what(*which)
    load_q.wait()
    load_go.wait()

    def step(t, carry):
        for g in range(kv_heads):
            @pl.when(t // PAIRS == g)
            def _(g=g):
                for p in range(PAIRS):
                    now = [e for e in events if int(math.floor(e[0])) == g * PAIRS + p and e[0] >= 0]
                    if now:
                        @pl.when(lax.rem(t, PAIRS) == p)
                        def _(now=now):
                            for _, what, which in now:
                                what(*which)
        pair(t // PAIRS, lax.rem(t, PAIRS))
        return carry

    lax.fori_loop(0, n, step, 0)
    for when, what, which in events:
        if when >= n:
            what(*which)

    for g in range(kv_heads):
        for d in range(1, SLOTS):
            near = d <= near_of(g)
            kv_copy(g, d - 1 if near else (0 if d == BACK else d + 1), d).wait_send()
            (d_near if near else d_far)(g, d).wait_send()


def local(n_dp, n_seq, queries, keys, values, d_out, doc_lengths):
    rows, width = queries.shape
    kv_width = keys.shape[1]
    kv_heads = kv_width // HEAD
    padded = -(-doc_lengths.shape[0] // 128) * 128
    lens = jnp.pad(doc_lengths, (0, padded - doc_lengths.shape[0])).reshape(1, padded)
    anywhere, vmem = pl.BlockSpec(memory_space=pl.ANY), pl.BlockSpec(memory_space=pltpu.VMEM)
    dma = pltpu.SemaphoreType.DMA
    bf16, f32 = jnp.bfloat16, jnp.float32
    return pl.pallas_call(
        functools.partial(kernel, kv_heads, n_dp, n_seq),
        out_shape=(
            jax.ShapeDtypeStruct((rows, width), bf16),
            jax.ShapeDtypeStruct((rows, kv_width), bf16),
            jax.ShapeDtypeStruct((rows, kv_width), bf16),
        ),
        in_specs=[anywhere] * 4 + [vmem],
        out_specs=(vmem, vmem, vmem),
        scratch_shapes=[
            pltpu.VMEM((rows, width), bf16),
            pltpu.VMEM((rows, width), bf16),
            pltpu.VMEM((kv_heads, 2, SLOTS, ROWS, HEAD), bf16),
            pltpu.VMEM((HEAD, SLOTS * ROWS), bf16),
            pltpu.VMEM((SLOTS, ROWS, ROWS), f32),
            pltpu.VMEM((SLOTS * ROWS, 2 * ROWS), f32),
            pltpu.VMEM((SLOTS * ROWS, 2 * ROWS), f32),
            pltpu.VMEM((kv_heads, 2, SLOTS, ROWS, HEAD), f32),
            pltpu.VMEM((kv_heads, SLOTS, 2, ROWS, HEAD), bf16),
            pltpu.VMEM((kv_heads, SLOTS + 1, 2, ROWS, HEAD), bf16),
            dma((2,)),
            dma((kv_heads, 2)),
            dma((kv_heads, SLOTS)),
            dma((kv_heads, SLOTS)),
            dma((kv_heads, SLOTS)),
            dma((kv_heads, SLOTS + 1)),
        ],
        compiler_params=pltpu.CompilerParams(
            collective_id=0, has_side_effects=True, vmem_limit_bytes=48 * 2**20
        ),
        cost_estimate=pl.CostEstimate(flops=4_700_000_000, bytes_accessed=4_000_000, transcendentals=3_700_000),
    )(queries, keys, values, d_out, lens)


def solution(mesh):
    rows = P(("dp", "seq"), None)
    return jax.shard_map(
        functools.partial(local, mesh.shape["dp"], mesh.shape["seq"]),
        mesh=mesh, in_specs=(rows, rows, rows, rows, P()), out_specs=(rows, rows, rows), check_vma=False)
```

time: 373 us -> 97.9 us (0.26)
  the two profiles are of different devices: /device:TPU:448 before, /device:TPU:8 now
where the time goes in v1:
time: 97.9 us; the launch traced here: 97.6 us
  Pallas kernels  89.8 us (92%)
  local copies, waits for them, and re-layouts  7.22 us (7%)
    pallas_call x1, Pallas kernels, local(): pl.pallas_call(functools.partial(kernel, kv_heads, n_dp, n_seq), out_shap...  89.8 us
    unnamed x11, local copies, waits for them, and re-layouts  6.54 us

profile of v1, /device:TPU:8, one launch (start us, length us, event | category | flops | bytes accessed | tf_op | source)
XLA Modules:
  0.0 97.6 jit_solution(14258355779598010031)
XLA Ops:
  0.6 0.7 pad.4
  1.3 0.0 copy-start
  1.3 1.2 %copy-done = bf16[128,4096]{1,0:T(8,128)(2,1)S(1)} copy-done((bf16[128,4096]{1,0:T(8,128)(2,1)S(1)}, bf16[128,4096]{1,0:T(8,128)(2,1)}, u32[]{:S(2)}) %copy-start) | copy-done | bytes 1048600
  2.5 0.0 copy-start.1
  2.5 1.2 %copy-done.1 = bf16[128,4096]{1,0:T(8,128)(2,1)S(1)} copy-done((bf16[128,4096]{1,0:T(8,128)(2,1)S(1)}, bf16[128,4096]{1,0:T(8,128)(2,1)}, u32[]{:S(2)}) %copy-start.1) | copy-done | bytes 1048600
  3.8 0.0 copy-start.2
  3.8 0.9 copy-done.2
  4.7 0.0 copy-start.3
  4.7 0.9 copy-done.3
  5.6 89.8 %shard_map.76 = (bf16[128,4096]{1,0:T(8,128)(2,1)S(1)}, bf16[128,512]{1,0:T(8,128)(2,1)S(1)}, bf16[128,512]{1,0:T(8,128)(2,1)S(1)}) custom-call(bf16[128,4096]{1,0:T(8,128)(2,1)S(1)} %copy-done, bf16[128,512]{1,0:T(8,128)(2,1)S(1)} %copy-done.2, bf16[128,512]{1,0:T(8,128)(2,1)S(1)} %copy-done.3, bf16[128,4096]{1,0:T(8,128)(2,1)S(1)} %copy-done.1, ...), custom_call_target="tpu_custom_call" | custom-call | flops 4700000256 | bytes 4000000 | tf_op jit(solution)/shard_map/pallas_call | solution.py:225
  95.4 1.0 copy.11
  96.3 0.7 copy.12
  97.0 0.7 copy.13
Async XLA Ops:
  1.3 1.2 %copy-start = (bf16[128,4096]{1,0:T(8,128)(2,1)S(1)}, bf16[128,4096]{1,0:T(8,128)(2,1)}, u32[]{:S(2)}) copy-start(bf16[128,4096]{1,0:T(8,128)(2,1)} %q_hbm.1) | copy-start | bytes 3145732
  2.5 1.2 %copy-start.1 = (bf16[128,4096]{1,0:T(8,128)(2,1)S(1)}, bf16[128,4096]{1,0:T(8,128)(2,1)}, u32[]{:S(2)}) copy-start(bf16[128,4096]{1,0:T(8,128)(2,1)} %go_hbm.1) | copy-start | bytes 3145732
  3.8 0.9 copy-start.2
  4.7 0.9 copy-start.3

commit v2 on v1

v2 whole, which is shorter than its diff:
```python
import functools
import math

import jax
import jax.numpy as jnp
from jax import lax
from jax.experimental import pallas as pl
from jax.experimental.pallas import tpu as pltpu
from jax.sharding import PartitionSpec as P

HEAD = 128
GROUP = 8
ROWS = 128
BACK = 6
SLOTS = BACK + 1
PAIRS = GROUP // 2
MESH = pl.DeviceIdType.MESH
NEG = -1e30
CONTRACT_LAST = (((1,), (1,)), ((), ()))


NEAR = 3
SCHEDULE = (
    (("kf", 0), ("kf", 1), ("kn", 0, 1), ("kn", 1, 1), ("kx", 0, 6), ("kf", 2), ("kn", 0, 2), ("kx", 1, 6), ("kn", 1, 2), ("kx", 0, 5), ("kn", 2, 1), ("kn", 0, 3), ("kx", 2, 6), ("kn", 1, 3), ("kx", 1, 5), ("kf", 3), ("kn", 2, 2), ("kx", 0, 4),),
    (("kx", 2, 5),),
    (("kn", 3, 1),),
    (("kx", 1, 4), ("kn", 2, 3),),
    (("df", 0),),
    (),
    (("kx", 3, 6), ("kn", 3, 2), ("kx", 2, 4),),
    (),
    (("df", 1), ("dn", 0, 2), ("dx", 0, 5),),
    (("kx", 3, 5), ("kn", 3, 3),),
    (),
    (("dn", 1, 2), ("dx", 1, 5), ("dn", 0, 1), ("dx", 0, 6), ("kx", 3, 4),),
    (("df", 2), ("dn", 1, 1), ("dx", 1, 6),),
    (),
    (),
    (),
    (("df", 3), ("dd", 0), ("dn", 2, 2), ("dx", 2, 5), ("dd", 1), ("dn", 3, 2), ("dx", 3, 5), ("dn", 2, 1), ("dx", 2, 6), ("dn", 3, 1), ("dx", 3, 6), ("dd", 2), ("dd", 3),),
)


def kernel(
    kv_heads, n_dp, n_seq,
    q_hbm, k_hbm, v_hbm, go_hbm, len_ref,
    dq_ref, dk_ref, dv_ref,
    q_ref, go_ref, kv, kt, bias, s_a, g_a, top_a, s_b, g_b, top_b, part, out_buf, in_buf,
    load_sem, own_sem, kv_send, kv_recv, d_send, d_recv,
):
    total = n_dp * n_seq
    me = lax.axis_index("dp") * n_seq + lax.axis_index("seq")

    def device(offset):
        there = lax.rem(me + (offset + total), total)
        return (there // n_seq, lax.rem(there, n_seq))

    own = []
    for g in range(kv_heads):
        for which, ref in ((0, k_hbm), (1, v_hbm)):
            own.append(pltpu.make_async_copy(
                ref.at[:, pl.ds(g * HEAD, HEAD)], kv.at[g, 0, which], own_sem.at[g, which]))
            own[-1].start()
    load_q = pltpu.make_async_copy(q_hbm, q_ref, load_sem.at[0])
    load_go = pltpu.make_async_copy(go_hbm, go_ref, load_sem.at[1])
    load_q.start()
    load_go.start()

    barrier = pltpu.get_barrier_semaphore()
    partners = (1, -1, BACK, -BACK)
    for offset in partners:
        pl.semaphore_signal(barrier, inc=1, device_id=device(offset), device_id_type=MESH)

    pl.semaphore_wait(barrier, len(partners))

    def kv_copy(g, source, target):
        offset = {(0, BACK): BACK}.get((source, target), target - source)
        return pltpu.make_async_remote_copy(
            src_ref=kv.at[g, source], dst_ref=kv.at[g, target],
            send_sem=kv_send.at[g, target], recv_sem=kv_recv.at[g, target],
            device_id=device(offset), device_id_type=MESH)

    def kv_first(g):
        own[2 * g].wait()
        own[2 * g + 1].wait()
        kv_copy(g, 0, 1).start()
        kv_copy(g, 0, BACK).start()

    def kv_near(g, d):
        kv_copy(g, d - 1, d).wait_recv()
        if d < NEAR:
            kv_copy(g, d, d + 1).start()

    def kv_far(g, d):
        kv_copy(g, 0 if d == BACK else d + 1, d).wait_recv()
        if d > NEAR + 1:
            kv_copy(g, d, d - 1).start()

    def d_copy(g, source, target, offset):
        return pltpu.make_async_remote_copy(
            src_ref=out_buf.at[g, source], dst_ref=in_buf.at[g, target],
            send_sem=d_send.at[g, source], recv_sem=d_recv.at[g, target],
            device_id=device(offset), device_id_type=MESH)

    def d_near(g, d):
        return d_copy(g, d, d - 1, -1)

    def d_far(g, d):
        return d_copy(g, d, d + 1, 1 if d < BACK else -BACK)

    def d_first(g):
        for d, copy in ((NEAR, d_near), (NEAR + 1, d_far)):
            out_buf[g, d] = part[g, :, d].astype(jnp.bfloat16)
            copy(g, d).start()

    def add_on(g, d):
        out_buf[g, d] = (part[g, :, d] + in_buf[g, d].astype(jnp.float32)).astype(jnp.bfloat16)

    def d_pass_near(g, d):
        d_near(g, d + 1).wait_recv()
        add_on(g, d)
        d_near(g, d).start()

    def d_pass_far(g, d):
        d_far(g, d - 1).wait_recv()
        add_on(g, d)
        d_far(g, d).start()

    def d_done(g):
        d_near(g, 1).wait_recv()
        d_far(g, BACK).wait_recv()
        done = part[g, :, 0] + in_buf[g, 0].astype(jnp.float32) + in_buf[g, BACK + 1].astype(jnp.float32)
        dk_ref[:, g * HEAD:(g + 1) * HEAD] = done[0].astype(jnp.bfloat16)
        dv_ref[:, g * HEAD:(g + 1) * HEAD] = done[1].astype(jnp.bfloat16)

    acts = {"kf": kv_first, "kn": kv_near, "kx": kv_far,
            "df": d_first, "dn": d_pass_near, "dx": d_pass_far, "dd": d_done}

    def act(slot):
        for kind, *which in slot:
            acts[kind](*which)

    scale = 1.0 / math.sqrt(HEAD)
    exp_scale = scale / math.log(2.0)

    def flat(x):
        return x.reshape(SLOTS * ROWS, x.shape[-1])

    def heads_of(ref, at):
        return jnp.concatenate([ref[:, pl.ds(at, HEAD)], ref[:, pl.ds(at + HEAD, HEAD)]], axis=0)

    def place(t):
        return t // PAIRS, pl.multiple_of(t * (2 * HEAD), 2 * HEAD)

    def products(t, s_ref, g_ref, top_ref):
        g, at = place(t)
        off = flat(bias[...])
        s = lax.dot_general(flat(kv[g, :, 0]), heads_of(q_ref, at), CONTRACT_LAST, preferred_element_type=jnp.float32)
        s = s + jnp.concatenate([off, off], axis=1)
        s_ref[...] = s
        top_ref[...] = jnp.max(s, axis=0, keepdims=True)
        g_ref[...] = lax.dot_general(
            flat(kv[g, :, 1]), heads_of(go_ref, at), CONTRACT_LAST, preferred_element_type=jnp.float32)

    def finish(t, s_ref, g_ref, top_ref):
        g, at = place(t)
        q2, go2 = heads_of(q_ref, at), heads_of(go_ref, at)
        e = jnp.exp2((s_ref[...] - top_ref[...]) * exp_scale)
        s_ref[...] = e
        inv = 1.0 / jnp.sum(e, axis=0, keepdims=True)
        delta = jnp.sum(e * g_ref[...], axis=0, keepdims=True) * inv
        e = s_ref[...]
        low = (e * inv).astype(jnp.bfloat16)
        ds = ((e * (inv * scale)) * (g_ref[...] - delta)).astype(jnp.bfloat16)
        dk = jnp.dot(ds, q2, preferred_element_type=jnp.float32)
        dv = jnp.dot(low, go2, preferred_element_type=jnp.float32)
        part[g, 0] += dk.reshape(SLOTS, ROWS, HEAD)
        part[g, 1] += dv.reshape(SLOTS, ROWS, HEAD)
        dq = jnp.dot(kt[g], ds, preferred_element_type=jnp.float32).T.astype(jnp.bfloat16)
        dq_ref[:, pl.ds(at, HEAD)] = dq[:ROWS]
        dq_ref[:, pl.ds(at + HEAD, HEAD)] = dq[ROWS:]

    starts = 0
    while SCHEDULE[0][starts][0] == "kf":
        starts += 1
    act(SCHEDULE[0][:starts])

    lens = len_ref[...].astype(jnp.float32)
    n_len = lens.shape[1]
    j = lax.broadcasted_iota(jnp.int32, (n_len, n_len), 0)
    k = lax.broadcasted_iota(jnp.int32, (n_len, n_len), 1)
    ends = jnp.sum(jnp.where(k <= j, jnp.broadcast_to(lens, (n_len, n_len)), 0.0), axis=1, keepdims=True)
    q_pos = (me * ROWS + lax.broadcasted_iota(jnp.int32, (1, ROWS), 1)).astype(jnp.float32)
    first = jnp.max(jnp.where(ends <= q_pos, ends, 0.0), axis=0, keepdims=True)
    for d in range(SLOTS):
        k_pos = ((me - d) * ROWS + lax.broadcasted_iota(jnp.int32, (ROWS, ROWS), 0)).astype(jnp.float32)
        bias[d] = jnp.where((k_pos >= first) & (k_pos <= q_pos), 0.0, NEG)
    part[...] = jnp.zeros_like(part)

    act(SCHEDULE[0][starts:])
    load_q.wait()
    load_go.wait()

    held = ((s_a, g_a, top_a), (s_b, g_b, top_b))
    n = kv_heads * PAIRS

    def events_of(t, parity):
        for p in range(parity, n, 2):
            if p and SCHEDULE[p]:
                @pl.when(t == p)
                def _(p=p):
                    act(SCHEDULE[p])

    def turn_keys(t):
        @pl.when(lax.rem(t, PAIRS) == 0)
        def _():
            kt[t // PAIRS] = flat(kv[t // PAIRS, :, 0]).T

    def step(u, carry):
        t = 2 * u
        events_of(t, 0)
        products(t + 1, *held[1])
        finish(t, *held[0])
        events_of(t + 1, 1)

        @pl.when(t + 2 < n)
        def _():
            turn_keys(t + 2)

        products(jnp.minimum(t + 2, n - 1), *held[0])
        finish(t + 1, *held[1])
        return carry

    turn_keys(0)
    products(0, *held[0])
    lax.fori_loop(0, n // 2, step, 0)
    act(SCHEDULE[-1])

    for g in range(kv_heads):
        for d in range(1, SLOTS):
            kv_copy(g, d - 1 if d <= NEAR else (0 if d == BACK else d + 1), d).wait_send()
            (d_near if d <= NEAR else d_far)(g, d).wait_send()


def write_out(a_ref, b_ref, c_ref, a_out, b_out, c_out, sem):
    pairs = ((a_ref, a_out), (b_ref, b_out), (c_ref, c_out))
    copies = [pltpu.make_async_copy(x, y, sem.at[i]) for i, (x, y) in enumerate(pairs)]
    for copy in copies:
        copy.start()
    for copy in copies:
        copy.wait()


def local(n_dp, n_seq, queries, keys, values, d_out, doc_lengths):
    rows, width = queries.shape
    kv_width = keys.shape[1]
    kv_heads = kv_width // HEAD
    lens = doc_lengths.reshape(1, -1)
    hbm, vmem = pl.BlockSpec(memory_space=pltpu.HBM), pl.BlockSpec(memory_space=pltpu.VMEM)
    dma = pltpu.SemaphoreType.DMA
    bf16, f32 = jnp.bfloat16, jnp.float32
    held = (
        pltpu.VMEM((SLOTS * ROWS, 2 * ROWS), f32),
        pltpu.VMEM((SLOTS * ROWS, 2 * ROWS), f32),
        pltpu.VMEM((1, 2 * ROWS), f32),
    )
    outs = (
        jax.ShapeDtypeStruct((rows, width), bf16),
        jax.ShapeDtypeStruct((rows, kv_width), bf16),
        jax.ShapeDtypeStruct((rows, kv_width), bf16),
    )
    made = pl.pallas_call(
        functools.partial(kernel, kv_heads, n_dp, n_seq),
        out_shape=outs,
        in_specs=[hbm] * 4 + [vmem],
        out_specs=(vmem, vmem, vmem),
        scratch_shapes=[
            pltpu.VMEM((rows, width), bf16),
            pltpu.VMEM((rows, width), bf16),
            pltpu.VMEM((kv_heads, SLOTS, 2, ROWS, HEAD), bf16),
            pltpu.VMEM((kv_heads, HEAD, SLOTS * ROWS), bf16),
            pltpu.VMEM((SLOTS, ROWS, ROWS), f32),
            *held,
            *held,
            pltpu.VMEM((kv_heads, 2, SLOTS, ROWS, HEAD), f32),
            pltpu.VMEM((kv_heads, SLOTS, 2, ROWS, HEAD), bf16),
            pltpu.VMEM((kv_heads, SLOTS + 1, 2, ROWS, HEAD), bf16),
            dma((2,)),
            dma((kv_heads, 2)),
            dma((kv_heads, SLOTS)),
            dma((kv_heads, SLOTS)),
            dma((kv_heads, SLOTS)),
            dma((kv_heads, SLOTS + 1)),
        ],
        compiler_params=pltpu.CompilerParams(
            collective_id=0, has_side_effects=True, vmem_limit_bytes=40 * 2**20
        ),
        cost_estimate=pl.CostEstimate(flops=4_700_000_000, bytes_accessed=4_000_000, transcendentals=3_700_000),
    )(*(pltpu.with_memory_space_constraint(x, pltpu.HBM) for x in (queries, keys, values, d_out)), lens)
    return pl.pallas_call(
        write_out,
        out_shape=outs,
        in_specs=[vmem] * 3,
        out_specs=(hbm,) * 3,
        scratch_shapes=[dma((3,))],
        compiler_params=pltpu.CompilerParams(vmem_limit_bytes=4 * 2**20),
    )(*made)


def solution(mesh):
    rows = P(("dp", "seq"), None)
    return jax.shard_map(
        functools.partial(local, mesh.shape["dp"], mesh.shape["seq"]),
        mesh=mesh, in_specs=(rows, rows, rows, rows, P()), out_specs=(rows, rows, rows), check_vma=False)
```

time: 97.9 us -> 75.4 us (0.77)
  the two profiles are of different devices: /device:TPU:8 before, /device:TPU:215 now
where the time goes in v2:
time: 75.4 us; the launch traced here: 75.2 us
  Pallas kernels  73.9 us (98%)
    pallas_call x1, Pallas kernels, local(): pl.pallas_call(functools.partial(kernel, kv_heads, n_dp, n_seq), out_shap...  72.9 us

profile of v2, /device:TPU:215, one launch (start us, length us, event | category | flops | bytes accessed | tf_op | source)
XLA Modules:
  0.0 75.2 jit_solution(13640654214275074920)
XLA Ops:
  0.6 0.0 copy-start
  0.6 0.7 copy-done
  1.3 72.9 %shard_map.76 = (bf16[128,4096]{1,0:T(8,128)(2,1)S(1)}, bf16[128,512]{1,0:T(8,128)(2,1)S(1)}, bf16[128,512]{1,0:T(8,128)(2,1)S(1)}) custom-call(bf16[128,4096]{1,0:T(8,128)(2,1)} %q_hbm.1, bf16[128,512]{1,0:T(8,128)(2,1)} %k_hbm.1, bf16[128,512]{1,0:T(8,128)(2,1)} %v_hbm.1, bf16[128,4096]{1,0:T(8,128)(2,1)} %go_hbm.1, s32[1,171]{1,0:T(1,128)S(1)} %bitcast.1), custom_call_target="tpu_custom_call" | custom-call | flops 4700000256 | bytes 4000000 | tf_op jit(solution)/shard_map/pallas_call | solution.py:272
  74.2 1.1 %shard_map.77 = (bf16[128,4096]{1,0:T(8,128)(2,1)}, bf16[128,512]{1,0:T(8,128)(2,1)}, bf16[128,512]{1,0:T(8,128)(2,1)}) custom-call(bf16[128,4096]{1,0:T(8,128)(2,1)S(1)} %get-tuple-element.6.a_ref, bf16[128,512]{1,0:T(8,128)(2,1)S(1)} %get-tuple-element.7.b_ref, bf16[128,512]{1,0:T(8,128)(2,1)S(1)} %get-tuple-element.8.c_ref), custom_call_target="tpu_custom_call" | custom-call | tf_op jit(solution)/shard_map/pallas_call | solution.py:300
Async XLA Ops:
  0.6 0.7 copy-start

commit v3 on v2

--- a/solution.py
+++ b/solution.py
@@ -19,33 +19,39 @@
 CONTRACT_LAST = (((1,), (1,)), ((), ()))
 
 
-NEAR = 3
+KV_FROM = (
+    (0, 1, 0, 3, 6, 0),
+    (0, 1, 2, 5, 6, 0),
+    (0, 1, 2, 5, 6, 0),
+    (0, 1, 2, 5, 6, 0),
+)
+NEAR_D = (4, 4, 3, 3)
 SCHEDULE = (
-    (("kf", 0), ("kf", 1), ("kn", 0, 1), ("kn", 1, 1), ("kx", 0, 6), ("kf", 2), ("kn", 0, 2), ("kx", 1, 6), ("kn", 1, 2), ("kx", 0, 5), ("kn", 2, 1), ("kn", 0, 3), ("kx", 2, 6), ("kn", 1, 3), ("kx", 1, 5), ("kf", 3), ("kn", 2, 2), ("kx", 0, 4),),
-    (("kx", 2, 5),),
-    (("kn", 3, 1),),
-    (("kx", 1, 4), ("kn", 2, 3),),
-    (("df", 0),),
+    (("kf", 0), ("kf", 1), ("kf", 2), ("kv", 0, 1), ("kv", 0, 6), ("kv", 1, 6), ("kv", 0, 3), ("kv", 1, 1), ("kv", 2, 1), ("kv", 2, 6), ("kv", 0, 2), ("kv", 0, 5), ("kf", 3), ("kv", 1, 5), ("kv", 0, 4),),
+    (("kv", 1, 2), ("kv", 2, 5),),
+    (("kv", 2, 2),),
+    (("kv", 3, 1), ("kv", 3, 6), ("kv", 1, 3), ("kv", 1, 4),),
+    (("df", 0), ("kv", 2, 3), ("kv", 2, 4),),
+    (("kv", 3, 2),),
+    (("kv", 3, 5),),
     (),
-    (("kx", 3, 6), ("kn", 3, 2), ("kx", 2, 4),),
+    (("df", 1), ("dn", 0, 3), ("dx", 0, 6), ("kv", 3, 3),),
+    (("kv", 3, 4),),
     (),
-    (("df", 1), ("dn", 0, 2), ("dx", 0, 5),),
-    (("kx", 3, 5), ("kn", 3, 3),),
+    (("dn", 1, 3), ("dx", 1, 6),),
+    (("df", 2), ("dn", 0, 2),),
     (),
-    (("dn", 1, 2), ("dx", 1, 5), ("dn", 0, 1), ("dx", 0, 6), ("kx", 3, 4),),
-    (("df", 2), ("dn", 1, 1), ("dx", 1, 6),),
+    (("dn", 1, 2),),
     (),
-    (),
-    (),
-    (("df", 3), ("dd", 0), ("dn", 2, 2), ("dx", 2, 5), ("dd", 1), ("dn", 3, 2), ("dx", 3, 5), ("dn", 2, 1), ("dx", 2, 6), ("dn", 3, 1), ("dx", 3, 6), ("dd", 2), ("dd", 3),),
+    (("df", 3), ("dn", 2, 2), ("dn", 0, 1), ("dx", 2, 5), ("dn", 1, 1), ("dn", 3, 2), ("dx", 3, 5), ("dn", 2, 1), ("dx", 2, 6), ("dd", 0), ("dd", 1), ("dx", 3, 6), ("dn", 3, 1), ("dd", 2), ("dd", 3),),
 )
 
 
 def kernel(
     kv_heads, n_dp, n_seq,
-    q_hbm, k_hbm, v_hbm, go_hbm, len_ref,
+    q_hbm, k_hbm, v_hbm, go_hbm, len_hbm,
     dq_ref, dk_ref, dv_ref,
-    q_ref, go_ref, kv, kt, bias, s_a, g_a, top_a, s_b, g_b, top_b, part, out_buf, in_buf,
+    q_ref, go_ref, len_ref, kv, kt, bias, s_a, g_a, top_a, s_b, g_b, top_b, part, out_buf, in_buf,
     load_sem, own_sem, kv_send, kv_recv, d_send, d_recv,
 ):
     total = n_dp * n_seq
@@ -54,6 +60,14 @@
     def device(offset):
         there = lax.rem(me + (offset + total), total)
         return (there // n_seq, lax.rem(there, n_seq))
+
+    barrier = pltpu.get_barrier_semaphore()
+    hops = {1, BACK}
+    for source in KV_FROM:
+        hops |= {abs(d - s) for d, s in zip(range(1, SLOTS), source)}
+    partners = sorted(hops | {-hop for hop in hops})
+    for offset in partners:
+        pl.semaphore_signal(barrier, inc=1, device_id=device(offset), device_id_type=MESH)
 
     own = []
     for g in range(kv_heads):
@@ -63,13 +77,10 @@
             own[-1].start()
     load_q = pltpu.make_async_copy(q_hbm, q_ref, load_sem.at[0])
     load_go = pltpu.make_async_copy(go_hbm, go_ref, load_sem.at[1])
+    load_len = pltpu.make_async_copy(len_hbm, len_ref, load_sem.at[2])
+    load_len.start()
     load_q.start()
     load_go.start()
-
-    barrier = pltpu.get_barrier_semaphore()
-    partners = (1, -1, BACK, -BACK)
-    for offset in partners:
-        pl.semaphore_signal(barrier, inc=1, device_id=device(offset), device_id_type=MESH)
 
     pl.semaphore_wait(barrier, len(partners))
 
@@ -80,21 +91,19 @@
             send_sem=kv_send.at[g, target], recv_sem=kv_recv.at[g, target],
             device_id=device(offset), device_id_type=MESH)
 
+    def kv_pass(g, source):
+        for d in range(1, SLOTS):
+            if KV_FROM[g][d - 1] == source:
+                kv_copy(g, source, d).start()
+
     def kv_first(g):
         own[2 * g].wait()
         own[2 * g + 1].wait()
-        kv_copy(g, 0, 1).start()
-        kv_copy(g, 0, BACK).start()
-
-    def kv_near(g, d):
-        kv_copy(g, d - 1, d).wait_recv()
-        if d < NEAR:
-            kv_copy(g, d, d + 1).start()
-
-    def kv_far(g, d):
-        kv_copy(g, 0 if d == BACK else d + 1, d).wait_recv()
-        if d > NEAR + 1:
-            kv_copy(g, d, d - 1).start()
+        kv_pass(g, 0)
+
+    def kv_take(g, d):
+        kv_copy(g, KV_FROM[g][d - 1], d).wait_recv()
+        kv_pass(g, d)
 
     def d_copy(g, source, target, offset):
         return pltpu.make_async_remote_copy(
@@ -109,7 +118,7 @@
         return d_copy(g, d, d + 1, 1 if d < BACK else -BACK)
 
     def d_first(g):
-        for d, copy in ((NEAR, d_near), (NEAR + 1, d_far)):
+        for d, copy in ((NEAR_D[g], d_near), (NEAR_D[g] + 1, d_far)):
             out_buf[g, d] = part[g, :, d].astype(jnp.bfloat16)
             copy(g, d).start()
 
@@ -133,7 +142,7 @@
         dk_ref[:, g * HEAD:(g + 1) * HEAD] = done[0].astype(jnp.bfloat16)
         dv_ref[:, g * HEAD:(g + 1) * HEAD] = done[1].astype(jnp.bfloat16)
 
-    acts = {"kf": kv_first, "kn": kv_near, "kx": kv_far,
+    acts = {"kf": kv_first, "kv": kv_take,
             "df": d_first, "dn": d_pass_near, "dx": d_pass_far, "dd": d_done}
 
     def act(slot):
@@ -185,6 +194,7 @@
         starts += 1
     act(SCHEDULE[0][:starts])
 
+    load_len.wait()
     lens = len_ref[...].astype(jnp.float32)
     n_len = lens.shape[1]
     j = lax.broadcasted_iota(jnp.int32, (n_len, n_len), 0)
@@ -238,8 +248,8 @@
 
     for g in range(kv_heads):
         for d in range(1, SLOTS):
-            kv_copy(g, d - 1 if d <= NEAR else (0 if d == BACK else d + 1), d).wait_send()
-            (d_near if d <= NEAR else d_far)(g, d).wait_send()
+            kv_copy(g, KV_FROM[g][d - 1], d).wait_send()
+            (d_near if d <= NEAR_D[g] else d_far)(g, d).wait_send()
 
 
 def write_out(a_ref, b_ref, c_ref, a_out, b_out, c_out, sem):
@@ -272,11 +282,12 @@
     made = pl.pallas_call(
         functools.partial(kernel, kv_heads, n_dp, n_seq),
         out_shape=outs,
-        in_specs=[hbm] * 4 + [vmem],
+        in_specs=[hbm] * 5,
         out_specs=(vmem, vmem, vmem),
         scratch_shapes=[
             pltpu.VMEM((rows, width), bf16),
             pltpu.VMEM((rows, width), bf16),
+            pltpu.VMEM(lens.shape, jnp.int32),
             pltpu.VMEM((kv_heads, SLOTS, 2, ROWS, HEAD), bf16),
             pltpu.VMEM((kv_heads, HEAD, SLOTS * ROWS), bf16),
             pltpu.VMEM((SLOTS, ROWS, ROWS), f32),
@@ -285,7 +296,7 @@
             pltpu.VMEM((kv_heads, 2, SLOTS, ROWS, HEAD), f32),
             pltpu.VMEM((kv_heads, SLOTS, 2, ROWS, HEAD), bf16),
             pltpu.VMEM((kv_heads, SLOTS + 1, 2, ROWS, HEAD), bf16),
-            dma((2,)),
+            dma((3,)),
             dma((kv_heads, 2)),
             dma((kv_heads, SLOTS)),
             dma((kv_heads, SLOTS)),
@@ -296,7 +307,7 @@
             collective_id=0, has_side_effects=True, vmem_limit_bytes=40 * 2**20
         ),
         cost_estimate=pl.CostEstimate(flops=4_700_000_000, bytes_accessed=4_000_000, transcendentals=3_700_000),
-    )(*(pltpu.with_memory_space_constraint(x, pltpu.HBM) for x in (queries, keys, values, d_out)), lens)
+    )(*(pltpu.with_memory_space_constraint(x, pltpu.HBM) for x in (queries, keys, values, d_out, lens)))
     return pl.pallas_call(
         write_out,
         out_shape=outs,

time: 75.4 us -> 70.8 us (0.939)
  the two profiles are of different devices: /device:TPU:215 before, /device:TPU:8 now
where the time goes in v3:
time: 70.8 us; the launch traced here: 70.7 us
  Pallas kernels  70 us (99%)
    pallas_call x1, Pallas kernels, local(): pl.pallas_call(functools.partial(kernel, kv_heads, n_dp, n_seq), out_shap...  68.9 us

profile of v3, /device:TPU:8, one launch (start us, length us, event | category | flops | bytes accessed | tf_op | source)
XLA Modules:
  0.0 70.7 jit_solution(14138368330812150077)
XLA Ops:
  0.6 68.9 %shard_map.76 = (bf16[128,4096]{1,0:T(8,128)(2,1)S(1)}, bf16[128,512]{1,0:T(8,128)(2,1)S(1)}, bf16[128,512]{1,0:T(8,128)(2,1)S(1)}) custom-call(bf16[128,4096]{1,0:T(8,128)(2,1)} %q_hbm.1, bf16[128,512]{1,0:T(8,128)(2,1)} %k_hbm.1, bf16[128,512]{1,0:T(8,128)(2,1)} %v_hbm.1, bf16[128,4096]{1,0:T(8,128)(2,1)} %go_hbm.1, s32[1,171]{1,0:T(1,128)} %bitcast.1), custom_call_target="tpu_custom_call" | custom-call | flops 4700000256 | bytes 4000000 | tf_op jit(solution)/shard_map/pallas_call | solution.py:282
  69.6 1.1 %shard_map.77 = (bf16[128,4096]{1,0:T(8,128)(2,1)}, bf16[128,512]{1,0:T(8,128)(2,1)}, bf16[128,512]{1,0:T(8,128)(2,1)}) custom-call(bf16[128,4096]{1,0:T(8,128)(2,1)S(1)} %get-tuple-element.6.a_ref, bf16[128,512]{1,0:T(8,128)(2,1)S(1)} %get-tuple-element.7.b_ref, bf16[128,512]{1,0:T(8,128)(2,1)S(1)} %get-tuple-element.8.c_ref), custom_call_target="tpu_custom_call" | custom-call | tf_op jit(solution)/shard_map/pallas_call | solution.py:311
